TPU v7x, 32 devices: a whole 2x2x4 slice. The times are simulated.
32 devices in a mesh: lat: 4 (over z), lon: 4 (over y, x), ens: 2 (over core).
Axes of the slice: x: 2, y: 2, z: 4, core: 2. Of those that a mesh axis runs over, the one named last changes fastest.
Arguments:
- band_field: bfloat16 [256, 256, 360], P(('ens', 'lat'), 'lon'), parts along dimension 0, may hold values from -6 to 6
- offsets: int32 [128, 4], P('lat'), may hold values from -3 to 3, as said below
- live_counts: int32 [128], P('lat'), may hold values from 1 to 4, as said below
- band_ids: int32 [128, 4], P('lat'), may hold values from 0 to 7
- tap_bank: bfloat16 [9, 8, 128], replicated, as said below
- mixing: bfloat16 [9, 64, 256], replicated, may hold values from -0.25 to 0.25
Outputs:
- convolved: bfloat16 [256, 360, 256], P(('ens', 'lat'), 'lon'), parts along dimension 0
There are 2 independent parts, one for each index of `ens`. A program takes and returns all parts, laid end to end along the dimension named above; an argument that names none is the same for every part. Nothing has to cross between parts.
Inputs may be any that keep to these rules, and one draw needn't show every extreme that they name: Row i + offsets[i, s] lies in the grid of 128 rows; offsets[i, 0] is 0; offsets of -3 and +3 both occur. Slots s >= live_counts[i] of row i are unused. tap_bank[k, b, d] is zero unless -r <= d - 64 < r, with r = (64 * (b + 1)) // 8.
All inputs are finite; a program needn't handle non-finite values.
Results may differ from a plain program's by a relative error of at most 0.0049.
Values may be sent and summed in bfloat16 or wider, within the bound.
A program may use at most 128 MiB of HBM per device.

v0:
```python
import jax
import jax.numpy as jnp
from jax import lax
from jax.sharding import PartitionSpec as P

GROUPS = 4
BASIS = 9
REACH = 64
HALO = 3
SLOTS = 4


def extended_2(x, sides, width, wrap):
    for axis, dim in sides:
        size, length = (lax.axis_size(axis), x.shape[dim])
        up = [(i, (i + 1) % size) for i in range(size if wrap else size - 1)]
        down = [(j, i) for i, j in up]
        last = lax.slice_in_dim(x, length - width, length, axis=dim)
        first = lax.slice_in_dim(x, 0, width, axis=dim)
        before = lax.ppermute(last, axis, up)
        after = lax.ppermute(first, axis, down)
        x = jnp.concatenate([before, x, after], axis=dim)
    return x


def on_device(band_field, offsets, live_counts, band_ids, tap_bank, mixing):
    tiles = lax.all_to_all(band_field, "lon", split_axis=2, concat_axis=1, tiled=True)
    widened = extended_2(tiles, (("lon", 2),), REACH, True)
    extended = extended_2(widened, (("lat", 0),), HALO, False)
    channels = extended.shape[1]
    span_cells = extended.shape[2]
    lon_cells = span_cells - 2 * REACH
    group_width = channels // GROUPS
    mixing_split = mixing.reshape(BASIS, group_width, GROUPS, group_width)
    distance = lax.broadcasted_iota(jnp.int32, (span_cells, lon_cells), 0) - lax.broadcasted_iota(
        jnp.int32, (span_cells, lon_cells), 1
    )
    inside = (distance >= 0) & (distance < 2 * REACH)
    picked = jnp.take(tap_bank, jnp.clip(distance, 0, 2 * REACH - 1), axis=2)
    toeplitz = jnp.where(inside, picked, jnp.zeros((), tap_bank.dtype))

    def slot_term(row_index, offset, band_index):
        source = lax.dynamic_index_in_dim(extended, row_index + HALO + offset, 0, keepdims=False)
        matrix = lax.dynamic_index_in_dim(toeplitz, band_index, 1, keepdims=False)
        return jnp.einsum("cj,kjl->kcl", source, matrix, preferred_element_type=jnp.float32)

    def one_row(packed):
        row_index, offset_row, live_count, band_row = packed
        summed = jnp.zeros((BASIS, channels, lon_cells), jnp.float32)
        for slot_index in range(SLOTS):
            live_mask = (slot_index < live_count).astype(jnp.float32)
            summed = summed + live_mask * slot_term(
                row_index, offset_row[slot_index], band_row[slot_index]
            )
        quadrature = summed.astype(jnp.bfloat16).reshape(BASIS, GROUPS, group_width, lon_cells)
        mixed_rows = jnp.einsum(
            "kcgo,kgcl->lgo", mixing_split, quadrature, preferred_element_type=jnp.float32
        )
        return mixed_rows.reshape(lon_cells, channels).astype(jnp.bfloat16)

    local_rows = jnp.arange(offsets.shape[0], dtype=jnp.int32)
    return lax.map(one_row, (local_rows, offsets, live_counts, band_ids))


def solution(mesh):
    placed = (P(("ens", "lat"), "lon", None), P("lat", None), P("lat"), P("lat", None), P(), P())
    return jax.shard_map(
        on_device,
        mesh=mesh,
        in_specs=placed,
        out_specs=P(("ens", "lat"), "lon", None),
        check_vma=False,
    )
```

profile of v0, /device:TPU:0, one launch (start us, length us, event | category | flops | bytes accessed | tf_op | source)
XLA Modules:
  0.0 895.0 jit_solution(11943615960658329803)
XLA Ops:
  0.0 5.8 copy.22
  5.8 3.2 reshape.100
  9.0 24.1 %all_to_all.18 = bf16[4,2,92160]{2,1,0:T(2,128)(2,1)S(1)} all-to-all(bf16[4,2,92160]{2,1,0:T(2,128)(2,1)} %reshape.100), channel_id=1, replica_groups=mesh['lat'=4,'lon'=4,'ens'=2] {'lon'}, dimensions={0} | all-to-all | bytes 2949120 | tf_op jit(solution)/shard_map/all_to_all | solution.py:27
  33.1 3.2 reshape.101
  36.3 3.9 copy.23
  40.2 2.8 fusion.34
  43.0 2.7 copy.25
  46.4 2.7 copy.24
  49.1 1.4 collective-permute-start
  50.9 51.4 %gather_fusion = bf16[19620,9,8]{1,2,0:T(8,128)(2,1)} fusion(bf16[9,8,128]{0,1,2:T(8,128)(2,1)S(1)} %copy.20, s32[20480]{0:T(1024)S(1)} %pad_clamp_fusion), kind=kCustom, calls=%fused_computation | custom fusion | bytes 5729040 | tf_op jit(solution)/shard_map/jit(_take)/gather | solution.py:39
  102.3 36.8 %copy.32 = bf16[218,90,9,8]{1,0,3,2:T(8,128)(2,1)} copy(bf16[218,90,9,8]{2,3,1,0:T(8,128)(2,1)} %bitcast.125) | data formatting | bytes 5650560 | tf_op jit(solution)/shard_map/jit(_take)/gather | solution.py:39
  139.2 2.8 copy.27
  141.9 2.8 copy.26
  144.7 2.7 pad_maximum_fusion.3
  148.8 4.8 collective-permute-start.2
  153.5 2.4 select_bitcast_fusion
  155.9 6.4 copy.28
  163.6 6.7 pad_maximum_fusion
  170.3 7.3 copy.29
  177.7 713.1 %while.10 = (s32[]{:T(128)}, bf16[32,90,256]{1,2,0:T(8,128)(2,1)}, s32[32]{0:T(128)S(1)}, s32[32,4]{0,1:T(4,128)S(1)}, bf16[9,8,218,90]{2,3,0,1:T(8,128)(2,1)}, ...) while((s32[]{:T(128)}, bf16[32,90,256]{1,2,0:T(8,128)(2,1)}, ...), condition=%wide.region_1.2_spmd, body=%wide.region_0.1_spmd.sunk | while | flops 389859840 | bytes 9319145 | solution.py:62
  192.9 1.3 fusion.66
  215.1 1.3 fusion.66
  237.4 1.3 fusion.66
  250.8 1.3 convolution_multiply_fusion.5
  259.7 1.3 fusion.66
  282.0 1.3 fusion.66
  322.2 1.3 fusion.65
  344.5 1.3 fusion.65
  362.2 1.3 convolution_multiply_fusion.5
  389.1 1.3 fusion.65
  397.9 1.3 fusion.67
  411.4 1.3 fusion.65
  429.0 1.3 convolution_multiply_fusion.5
  482.5 1.3 fusion.66
  522.8 1.3 fusion.65
  545.1 1.3 fusion.65
  571.7 1.3 fusion.66
  585.0 1.3 convolution_multiply_fusion.5
  611.9 1.3 fusion.65
  620.7 1.3 fusion.67
  638.5 1.3 fusion.66
  651.9 1.3 convolution_multiply_fusion.5
  678.8 1.3 fusion.65
  687.6 1.3 fusion.67
  696.4 1.3 convolution_multiply_fusion.5
  763.3 1.3 convolution_multiply_fusion.5
  861.3 1.3 fusion.66
  890.7 4.3 copy.31
  (381 shorter events, 254.4 us)
Async XLA Ops:
  43.0 7.4 copy-start.3
  45.7 93.4 %collective-permute-start.1 = (bf16[32,256,64]{1,2,0:T(8,128)(2,1)}, bf16[32,256,64]{1,2,0:T(8,128)(2,1)}, u32[]{:S(2)}, u32[]{:S(2)}) collective-permute-start(bf16[32,256,64]{1,2,0:T(8,128)(2,1)} %copy.25), channel_id=1, source_target_pairs={{2,0},{4,2},{6,4},{0,6},{3,1},{5,3},{7,5},{1,7},{10,8},{12,10},{14... | collective-permute-start | bytes 3145736 | tf_op jit(solution)/shard_map/ppermute | solution.py:21
  49.1 92.8 %collective-permute-start = (bf16[32,256,64]{1,2,0:T(8,128)(2,1)}, bf16[32,256,64]{1,2,0:T(8,128)(2,1)}, u32[]{:S(2)}, u32[]{:S(2)}) collective-permute-start(bf16[32,256,64]{1,2,0:T(8,128)(2,1)} %copy.24), channel_id=1, source_target_pairs={{0,2},{2,4},{4,6},{6,0},{1,3},{3,5},{5,7},{7,1},{8,10},{10,12},{12... | collective-permute-start | bytes 3145736 | tf_op jit(solution)/shard_map/ppermute | solution.py:20
  144.7 8.8 copy-start
  147.5 16.1 %collective-permute-start.3 = (bf16[3,256,218]{2,1,0:T(8,128)(2,1)}, bf16[3,256,218]{2,1,0:T(8,128)(2,1)S(1)}, u32[]{:S(2)}, u32[]{:S(2)}) collective-permute-start(bf16[3,256,218]{2,1,0:T(8,128)(2,1)} %get-tuple-element.100), channel_id=1, source_target_pairs={{8,0},{16,8},{24,16},{9,1},{17,9},{25,17},{10,2},{18,10},{26,18},{... | collective-permute-start | bytes 1004552 | tf_op jit(solution)/shard_map/ppermute | solution.py:21
  148.8 14.9 %collective-permute-start.2 = (bf16[3,256,218]{2,1,0:T(8,128)(2,1)}, bf16[3,256,218]{2,1,0:T(8,128)(2,1)S(1)}, u32[]{:S(2)}, u32[]{:S(2)}) collective-permute-start(bf16[3,256,218]{2,1,0:T(8,128)(2,1)} %get-tuple-element.99), channel_id=1, source_target_pairs={{0,8},{8,16},{16,24},{1,9},{9,17},{17,25},{2,10},{10,18},{18,26},{... | collective-permute-start | bytes 1004552 | tf_op jit(solution)/shard_map/ppermute | solution.py:20
  170.3 7.3 copy-start.1
  170.3 7.3 copy-start.2
  170.3 7.4 copy-start.4
where the time goes:
time: 905 us; the launch traced here: 895 us
  loops' own time  427 us (47%)
  local copies, waits for them, and re-layouts  247 us (27%)
  matrix products  177 us (20%)
  blocking collectives  24.1 us (3%)
  other arithmetic  11.9 us (1%)
    another operation x1, loops' own time, on_device(): return lax.map(one_row, (local_rows, offsets, live_counts, band_ids))  427 us
    dot_general x128, matrix products, slot_term(): jnp.einsum('cj,kjl->kcl', source, matrix, preferred_element_type=jnp.floa...  167 us
    gather x2, local copies, waits for them, and re-layouts, on_device(): picked = jnp.take(tap_bank, jnp.clip(distance, 0, 2 * REACH - 1), axis=2)  88.2 us
    dynamic_slice x96, local copies, waits for them, and re-layouts, on_device(): return lax.map(one_row, (local_rows, offsets, live_counts, band_ids))  41.3 us
    all_to_all x1, blocking collectives, on_device(): lax.all_to_all(band_field, 'lon', split_axis=2, concat_axis=1, tiled=True)  24.1 us
    dynamic_update_slice x32, local copies, waits for them, and re-layouts, on_device(): return lax.map(one_row, (local_rows, offsets, live_counts, band_ids))  20.3 us
    slice x32, local copies, waits for them, and re-layouts, one_row(): band_row[slot_index]  19.4 us
    while x4, local copies, waits for them, and re-layouts, on_device(): return lax.map(one_row, (local_rows, offsets, live_counts, band_ids))  19.3 us
  transfers between devices with their start and end apart: 4, of which 0 were waited for; matrix products, arithmetic and copies ran while one was open for 12% of the time, Pallas kernels for 0%

commit v1 on v0

--- a/solution.py
+++ b/solution.py
@@ -1,6 +1,10 @@
+import functools
+
 import jax
 import jax.numpy as jnp
 from jax import lax
+from jax.experimental import pallas as pl
+from jax.experimental.pallas import tpu as pltpu
 from jax.sharding import PartitionSpec as P
 
 GROUPS = 4
@@ -23,7 +27,7 @@
     return x
 
 
-def on_device(band_field, offsets, live_counts, band_ids, tap_bank, mixing):
+def tiled_plan(band_field, offsets, live_counts, band_ids, tap_bank, mixing):
     tiles = lax.all_to_all(band_field, "lon", split_axis=2, concat_axis=1, tiled=True)
     widened = extended_2(tiles, (("lon", 2),), REACH, True)
     extended = extended_2(widened, (("lat", 0),), HALO, False)
@@ -62,7 +66,90 @@
     return lax.map(one_row, (local_rows, offsets, live_counts, band_ids))
 
 
+NT=(((1,),(1,)),((),()))
+def kernel(R, mode, off_ref, live_ref, band_ref, xp_ref, taps_ref, m4_ref, out_ref, T_ref, W_ref, bd_ref, q_ref):
+    step = pl.program_id(0)
+    def window(r):
+        for t in range(4):
+            W_ref[r, t*64:(t+1)*64, :] = xp_ref[r, :, 90*t:90*t+256] if t < 3 else jnp.concatenate([xp_ref[r, :, 270:512], xp_ref[r,:,0:14]], axis=1)
+    @pl.when(step == 0)
+    def _():
+        def build(i, c):
+            row = jnp.broadcast_to(taps_ref[pl.ds(i, 1), :], (96, 256))
+            T_ref[i] = pltpu.roll(row, 0, 1, stride=1, stride_axis=0).astype(jnp.bfloat16)
+            return c
+        lax.fori_loop(0, 72, build, 0, unroll=4)
+        lane = lax.broadcasted_iota(jnp.int32, (64, 256), 1) // 64
+        for t in range(4):
+            for k in range(9):
+                bd_ref[k, t*64:(t+1)*64, :] = jnp.where(lane == t, m4_ref[k], jnp.zeros((), jnp.bfloat16))
+        def wb(r, c):
+            window(r); return c
+        lax.fori_loop(0, 38, wb, 0)
+    for r in range(R):
+        i = step * R + r
+        def slots(n):
+            acc = None
+            for s in range(n):
+                tb = T_ref[pl.ds(band_ref[i*4+s] * 9, 9)].reshape(864, 256)
+                if mode == 0:
+                    tb = jnp.where(s < live_ref[i], tb, jnp.zeros_like(tb))
+                d = lax.dot_general(tb, W_ref[i + 3 + off_ref[i*4+s]], NT, preferred_element_type=jnp.float32)
+                acc = d if acc is None else acc + d
+            q_ref[:, r*96:(r+1)*96, :] = acc.astype(jnp.bfloat16).reshape(9, 96, 256)
+        if mode == 0 or mode == 2:
+            slots(4)
+        else:
+            for n in range(1, 5):
+                pl.when(live_ref[i] == n)(functools.partial(slots, n))
+    acc = None
+    for k in range(9):
+        d = jnp.dot(q_ref[k], bd_ref[k], preferred_element_type=jnp.float32)
+        acc = d if acc is None else acc + d
+    low = lax.broadcasted_iota(jnp.int32, (96, 128), 1) < 64
+    for p in range(R//2):
+        a0 = acc[p*192:p*192+96]; a1 = acc[p*192+96:p*192+192]
+        for h in range(2):
+            b0 = a0[:, h*128:(h+1)*128]; b1 = a1[:, h*128:(h+1)*128]
+            out_ref[2*h, p] = jnp.where(low, b0, pltpu.roll(b1, 64, 1)).astype(jnp.bfloat16)
+            out_ref[2*h+1, p] = jnp.where(low, pltpu.roll(b0, 64, 1), b1).astype(jnp.bfloat16)
+
+def conv(off, live, band, xp, taps, m4, R=4, mode=1):
+    rows = live.shape[0]
+    sm = pl.BlockSpec(memory_space=pltpu.SMEM); vm = pl.BlockSpec(memory_space=pltpu.VMEM)
+    return pl.pallas_call(functools.partial(kernel, R, mode), grid=(rows//R,),
+        out_shape=jax.ShapeDtypeStruct((4, rows//2, 96, 128), jnp.bfloat16),
+        in_specs=[sm,sm,sm,vm,vm,vm],
+        out_specs=pl.BlockSpec((4, R//2, 96, 128), lambda s: (0, s, 0, 0)),
+        scratch_shapes=[pltpu.VMEM((72,96,256), jnp.bfloat16), pltpu.VMEM((rows+6,256,256), jnp.bfloat16),
+          pltpu.VMEM((9,256,256), jnp.bfloat16), pltpu.VMEM((9,R*96,256), jnp.bfloat16)],
+        compiler_params=pltpu.CompilerParams(vmem_limit_bytes=48*2**20),
+    )(off.reshape(-1), live, band.reshape(-1), xp, taps, m4)
+
+def grouped_plan(band_field, offsets, live_counts, band_ids, tap_bank, mixing):
+    rows = band_field.shape[0]
+    size = lax.axis_size("lat")
+    up = [(i, i + 1) for i in range(size - 1)]
+    before = lax.ppermute(band_field[rows - HALO:], "lat", up)
+    after = lax.ppermute(band_field[:HALO], "lat", [(j, i) for i, j in up])
+    x = jnp.concatenate([before, band_field, after], axis=0)
+    xp = jnp.concatenate([x[..., 360 - REACH:], x, x[..., :88]], axis=-1)
+    tp = jnp.pad(tap_bank.transpose(1, 0, 2).astype(jnp.float32), ((0, 0), (0, 0), (0, 128))).reshape(72, 256)
+    group = lax.axis_index("lon")
+    own = lax.dynamic_slice_in_dim(mixing, group * 64, 64, axis=2)
+    out = conv(offsets, live_counts, band_ids, xp, tp, jnp.tile(own, (1, 1, 4)))
+    got = lax.all_to_all(out, "lon", split_axis=0, concat_axis=0, tiled=True)
+    got = got[:, :, :90].reshape(4, rows // 2, 90, 2, 64)
+    return got.transpose(1, 3, 2, 0, 4).reshape(rows, 90, 256)
+
+
 def solution(mesh):
+    def on_device(*args):
+        field = args[0]
+        if field.shape[1] == 256 // GROUPS and field.shape[2] == 360 and mesh.shape["lon"] == 4 and field.shape[0] % 4 == 0:
+            return grouped_plan(*args)
+        return tiled_plan(*args)
+
     placed = (P(("ens", "lat"), "lon", None), P("lat", None), P("lat"), P("lat", None), P(), P())
     return jax.shard_map(
         on_device,

time: 905 us -> 79.2 us (0.09); the launches traced: 895 us -> 79 us
  loops' own time: 427 us -> 0 us
  local copies, waits for them, and re-layouts: 247 us -> 11.8 us
  matrix products: 177 us -> 0 us
  Pallas kernels: 0 us -> 32.6 us
  other arithmetic: 11.9 us -> 1.61 us
    another operation x1 -> x0, loops' own time: 427 us -> none  [on_device(): return lax.map(one_row, (local_rows, offsets, live_counts, band_ids))]
    dot_general x160 -> x0, matrix products: 177 us -> none  [the longest x128 167 us: slot_term(): jnp.einsum('cj,kjl->kcl', source, matrix, preferred_element_type=jnp.floa...]
    gather x2 -> x0, local copies, waits for them, and re-layouts: 88.2 us -> none  [on_device(): picked = jnp.take(tap_bank, jnp.clip(distance, 0, 2 * REACH - 1), axis=2)]
    dynamic_slice x96 -> x1, local copies, waits for them, and re-layouts: 41.3 us -> 0.11 us  [grouped_plan(): own = lax.dynamic_slice_in_dim(mixing, group * 64, 64, axis=2)]
    slice x67 -> x4, local copies, waits for them, and re-layouts: 45.3 us -> 4.5 us  [the longest x1 3.01 us: grouped_plan(): got = got[:, :, :90].reshape(4, rows // 2, 90, 2, 64)]
    pallas_call x0 -> x1, Pallas kernels: none -> 32.6 us  [conv(): pl.pallas_call(functools.partial(kernel, R, mode), grid=(rows // R,), out...]
    dynamic_update_slice x32 -> x0, local copies, waits for them, and re-layouts: 20.3 us -> none  [on_device(): return lax.map(one_row, (local_rows, offsets, live_counts, band_ids))]
    while x4 -> x0, local copies, waits for them, and re-layouts: 19.3 us -> none  [on_device(): return lax.map(one_row, (local_rows, offsets, live_counts, band_ids))]
  transfers between devices with their start and end apart: 4 -> 2, of which waited for: 0 -> 2; matrix products, arithmetic and copies ran while one was open for 12% -> 2% of each run, Pallas kernels for 0% -> 0%
where the time goes in v1:
time: 79.2 us; the launch traced here: 79 us
  Pallas kernels  32.6 us (41%)
  blocking collectives  22.2 us (28%)
  local copies, waits for them, and re-layouts  11.8 us (15%)
  starting transfers between devices  6.24 us (8%)
  waiting for transfers between devices  4.36 us (6%)
  other arithmetic  1.61 us (2%)
    pallas_call x1, Pallas kernels, conv(): pl.pallas_call(functools.partial(kernel, R, mode), grid=(rows // R,), out...  32.6 us
    all_to_all x1, blocking collectives, grouped_plan(): got = lax.all_to_all(out, 'lon', split_axis=0, concat_axis=0, tiled=True)  22.2 us
    ppermute x1, starting transfers between devices, grouped_plan(): before = lax.ppermute(band_field[rows - HALO:], 'lat', up)  4.94 us
    reshape x1, local copies, waits for them, and re-layouts, grouped_plan(): return got.transpose(1, 3, 2, 0, 4).reshape(rows, 90, 256)  4.28 us
    ppermute x1, waiting for transfers between devices, grouped_plan(): after = lax.ppermute(band_field[:HALO], 'lat', [(j, i) for i, j in up])  3.76 us
    slice x1, local copies, waits for them, and re-layouts, grouped_plan(): got = got[:, :, :90].reshape(4, rows // 2, 90, 2, 64)  3.01 us
    concatenate x1, other arithmetic, grouped_plan(): xp = jnp.concatenate([x[..., 360 - REACH:], x, x[..., :88]], axis=-1)  1.61 us
    transpose x1, local copies, waits for them, and re-layouts, grouped_plan(): return got.transpose(1, 3, 2, 0, 4).reshape(rows, 90, 256)  1.59 us
  transfers between devices with their start and end apart: 2, of which 2 were waited for; matrix products, arithmetic and copies ran while one was open for 2% of the time, Pallas kernels for 0%

profile of v1, /device:TPU:0, one launch (start us, length us, event | category | flops | bytes accessed | tf_op | source)
XLA Modules:
  0.0 79.0 jit_solution(17640671634996009333)
XLA Ops:
  0.0 0.0 copy-start
  0.0 0.0 copy-start.2
  0.0 0.0 copy-start.3
  0.0 0.0 copy-start.4
  0.0 0.0 copy-start.5
  0.0 1.1 %fusion = (bf16[3,64,360]{2,1,0:T(8,128)(2,1)S(1)}, bf16[3,64,360]{2,1,0:T(8,128)(2,1)S(1)}) fusion(bf16[32,64,360]{2,1,0:T(8,128)(2,1)} %param.6), kind=kLoop, calls=%fused_computation.6 | loop fusion | bytes 552960 | tf_op jit(solution)/shard_map/slice | solution.py:134
  1.2 4.9 %collective-permute-start = (bf16[3,64,360]{2,1,0:T(8,128)(2,1)S(1)}, bf16[3,64,360]{2,1,0:T(8,128)(2,1)S(1)}, u32[]{:S(2)}, u32[]{:S(2)}) collective-permute-start(bf16[3,64,360]{2,1,0:T(8,128)(2,1)S(1)} %get-tuple-element.6), channel_id=1, source_target_pairs={{0,8},{8,16},{16,24},{1,9},{9,17},{17,25},{2,10},{10,18},{18,26},{... | collective-permute-start | bytes 414728 | tf_op jit(solution)/shard_map/ppermute | solution.py:133
  6.1 1.3 %collective-permute-start.1 = (bf16[3,64,360]{2,1,0:T(8,128)(2,1)S(1)}, bf16[3,64,360]{2,1,0:T(8,128)(2,1)S(1)}, u32[]{:S(2)}, u32[]{:S(2)}) collective-permute-start(bf16[3,64,360]{2,1,0:T(8,128)(2,1)S(1)} %get-tuple-element.5), channel_id=1, source_target_pairs={{8,0},{16,8},{24,16},{9,1},{17,9},{25,17},{10,2},{18,10},{26,18},{... | collective-permute-start | bytes 414728 | tf_op jit(solution)/shard_map/ppermute | solution.py:134
  7.4 0.0 copy-done
  7.4 0.1 constant_dynamic-slice_fusion
  7.6 0.2 tile.4
  7.7 0.4 tile.10.m4_ref
  8.1 0.0 copy-done.3
  8.2 0.0 copy-done.4
  8.2 0.1 copy.11
  8.3 0.1 reshape.21.off_ref
  8.4 0.0 copy-done.5
  8.4 0.1 copy.12
  8.5 0.1 reshape.22.band_ref
  8.6 0.6 collective-permute-done
  9.2 0.0 copy-done.2
  9.2 0.3 constant_dynamic-update-slice_fusion.1
  9.6 3.8 %collective-permute-done.1 = bf16[3,64,360]{2,1,0:T(8,128)(2,1)S(1)} collective-permute-done((bf16[3,64,360]{2,1,0:T(8,128)(2,1)S(1)}, bf16[3,64,360]{2,1,0:T(8,128)(2,1)S(1)}, u32[]{:S(2)}, u32[]{:S(2)}) %collective-permute-start.1) | collective-permute-done | bytes 138272 | tf_op jit(solution)/shard_map/ppermute | solution.py:134
  13.4 0.2 slice.20
  13.6 0.1 slice.21
  13.7 0.0 copy-start.1
  13.7 1.6 %pad_maximum_fusion.xp_ref = bf16[38,64,512]{2,1,0:T(8,128)(2,1)S(1)} fusion(bf16[38,64,88]{2,1,0:T(8,128)(2,1)S(1)} %slice.21, bf16[38,64,360]{2,1,0:T(8,128)(2,1)S(1)} %constant_dynamic-update-slice_fusion, bf16[38,64,64]{2,1,0:T(8,128)(2,1)S(1)} %slice.20), kind=kLoop, calls=%fused_computation | loop fusion | flops 7471104 | bytes 4980736 | tf_op jit(solution)/shard_map/concatenate | solution.py:136
  15.3 0.0 copy-done.1
  15.3 32.6 %shard_map.64 = bf16[4,16,96,128]{3,2,1,0:T(8,128)(2,1)S(1)} custom-call(s32[128]{0:T(128)S(1)} %reshape.21.off_ref, s32[32]{0:T(128)S(1)} %copy-done.1, s32[128]{0:T(128)S(1)} %reshape.22.band_ref, bf16[38,64,512]{2,1,0:T(8,128)(2,1)S(1)} %pad_maximum_fusion.xp_ref, f32[72,256]{1,0:T(8,128)S(1)} %reshape.28.taps_ref, bf16[9,64,256]{2,1,0:T(8,128)(2,1)S(1)} %tile.10.m4_ref), custom_call_target="tpu_custom_call" | custom-call | tf_op jit(solution)/shard_map/pallas_call | solution.py:120
  48.0 22.2 %all_to_all.5 = bf16[4,16,96,128]{3,2,1,0:T(8,128)(2,1)} all-to-all(bf16[4,16,96,128]{3,2,1,0:T(8,128)(2,1)S(1)} %shard_map.64), channel_id=1, replica_groups=mesh['lat'=4,'lon'=4,'ens'=2] {'lon'}, dimensions={0} | all-to-all | bytes 3145728 | tf_op jit(solution)/shard_map/all_to_all | solution.py:141
  70.1 3.0 %copy.14 = bf16[4,16,90,128]{2,3,1,0:T(8,128)(2,1)S(1)} copy(bf16[4,16,90,128]{3,2,1,0:T(8,128)(2,1)} %bitcast.8) | data formatting | bytes 2949120 | tf_op jit(solution)/shard_map/slice | solution.py:142
  73.2 1.6 %copy.15 = bf16[16,2,90,4,64]{2,4,3,1,0:T(8,128)(2,1)} copy(bf16[16,2,90,4,64]{2,4,1,0,3:T(8,128)(2,1)S(1)} %bitcast.6) | data formatting | bytes 2949120 | tf_op jit(solution)/shard_map/transpose | solution.py:143
  74.7 4.3 %copy.16 = bf16[32,90,256]{2,0,1:T(8,128)(2,1)} copy(bf16[32,90,256]{1,2,0:T(8,128)(2,1)} %bitcast.7) | data formatting | bytes 2949120 | tf_op jit(solution)/shard_map/reshape | solution.py:143
  (5 shorter events, 0.1 us)
Async XLA Ops:
  0.0 7.4 %copy-start = (bf16[9,64,256]{2,1,0:T(8,128)(2,1)S(1)}, bf16[9,64,256]{2,1,0:T(8,128)(2,1)}, u32[]{:S(2)}) copy-start(bf16[9,64,256]{2,1,0:T(8,128)(2,1)} %param.11) | copy-start | bytes 884740
  0.0 9.2 %copy-start.2 = (bf16[32,64,360]{2,1,0:T(8,128)(2,1)S(1)}, bf16[32,64,360]{2,1,0:T(8,128)(2,1)}, u32[]{:S(2)}) copy-start(bf16[32,64,360]{2,1,0:T(8,128)(2,1)} %param.6) | copy-start | bytes 4423684
  0.0 8.1 %copy-start.3 = (bf16[9,8,128]{2,1,0:T(8,128)(2,1)S(1)}, bf16[9,8,128]{2,1,0:T(8,128)(2,1)}, u32[]{:S(2)}) copy-start(bf16[9,8,128]{2,1,0:T(8,128)(2,1)} %param.10) | copy-start | bytes 55300
  0.0 8.2 %copy-start.4 = (s32[32,4]{0,1:T(4,128)S(1)}, s32[32,4]{0,1:T(4,128)}, u32[]{:S(2)}) copy-start(s32[32,4]{0,1:T(4,128)} %param.7) | copy-start | bytes 1540
  0.0 8.4 %copy-start.5 = (s32[32,4]{0,1:T(4,128)S(1)}, s32[32,4]{0,1:T(4,128)}, u32[]{:S(2)}) copy-start(s32[32,4]{0,1:T(4,128)} %param.9) | copy-start | bytes 1540
  1.2 8.0 %collective-permute-start = (bf16[3,64,360]{2,1,0:T(8,128)(2,1)S(1)}, bf16[3,64,360]{2,1,0:T(8,128)(2,1)S(1)}, u32[]{:S(2)}, u32[]{:S(2)}) collective-permute-start(bf16[3,64,360]{2,1,0:T(8,128)(2,1)S(1)} %get-tuple-element.6), channel_id=1, source_target_pairs={{0,8},{8,16},{16,24},{1,9},{9,17},{17,25},{2,10},{10,18},{18,26},{... | collective-permute-start | bytes 414728 | tf_op jit(solution)/shard_map/ppermute | solution.py:133
  6.1 7.2 %collective-permute-start.1 = (bf16[3,64,360]{2,1,0:T(8,128)(2,1)S(1)}, bf16[3,64,360]{2,1,0:T(8,128)(2,1)S(1)}, u32[]{:S(2)}, u32[]{:S(2)}) collective-permute-start(bf16[3,64,360]{2,1,0:T(8,128)(2,1)S(1)} %get-tuple-element.5), channel_id=1, source_target_pairs={{8,0},{16,8},{24,16},{9,1},{17,9},{25,17},{10,2},{18,10},{26,18},{... | collective-permute-start | bytes 414728 | tf_op jit(solution)/shard_map/ppermute | solution.py:134
  13.7 1.6 %copy-start.1 = (s32[32]{0:T(128)S(1)}, s32[32]{0:T(128)}, u32[]{:S(2)}) copy-start(s32[32]{0:T(128)} %live_ref.1) | copy-start | bytes 388

commit v2 on v0

--- a/solution.py
+++ b/solution.py
@@ -1,6 +1,8 @@
 import jax
 import jax.numpy as jnp
 from jax import lax
+from jax.experimental import pallas as pl
+from jax.experimental.pallas import tpu as pltpu
 from jax.sharding import PartitionSpec as P
 
 GROUPS = 4
@@ -23,7 +25,7 @@
     return x
 
 
-def on_device(band_field, offsets, live_counts, band_ids, tap_bank, mixing):
+def tiled_plan(band_field, offsets, live_counts, band_ids, tap_bank, mixing):
     tiles = lax.all_to_all(band_field, "lon", split_axis=2, concat_axis=1, tiled=True)
     widened = extended_2(tiles, (("lon", 2),), REACH, True)
     extended = extended_2(widened, (("lat", 0),), HALO, False)
@@ -62,7 +64,176 @@
     return lax.map(one_row, (local_rows, offsets, live_counts, band_ids))
 
 
+NT = (((1,), (1,)), ((), ()))
+STEP = 4
+TILE = 90
+SPAN = 256
+LINES = 96
+
+
+def kernel(off_ref, live_ref, band_ref, x_ref, taps_ref, mix_ref, out_ref, bank, field, halo, weights, quad, send, recv, send_sem, recv_sem, halo_send, halo_recv):
+    me = lax.axis_index("lon")
+    lat = lax.axis_index("lat")
+    n_lat = lax.axis_size("lat")
+    rows = x_ref.shape[0]
+    steps = rows // STEP
+    above, below = lax.rem(lat + 1, n_lat), lax.rem(lat + n_lat - 1, n_lat)
+    partners = [lax.rem(me + d, 4) for d in range(1, 4)]
+    sources = [lax.rem(me + 4 - d, 4) for d in range(1, 4)]
+
+    barrier = pltpu.get_barrier_semaphore()
+    for p in partners:
+        pl.semaphore_signal(barrier, inc=1, device_id={"lon": p}, device_id_type=pl.DeviceIdType.MESH)
+    for q in (above, below):
+        pl.semaphore_signal(barrier, inc=1, device_id={"lat": q}, device_id_type=pl.DeviceIdType.MESH)
+
+    def window(x, slot):
+        for t in range(4):
+            s = (TILE * t - REACH) % 360
+            if s + SPAN > 360:
+                piece = jnp.concatenate([x[:, s:], x[:, : SPAN - 360 + s]], axis=1)
+            else:
+                piece = x[:, s : s + SPAN]
+            field[slot, t * 64 : (t + 1) * 64, :] = piece
+
+    def bank_block(i, c):
+        line = jnp.broadcast_to(taps_ref[pl.ds(i, 1), :], (LINES, SPAN))
+        bank[i] = pltpu.roll(line, 0, 1, stride=1, stride_axis=0).astype(jnp.bfloat16)
+        return c
+
+    lax.fori_loop(0, 72, bank_block, 0, unroll=4)
+    bank[72:81] = jnp.zeros((9, LINES, SPAN), jnp.bfloat16)
+    lane = lax.broadcasted_iota(jnp.int32, (64, SPAN), 1) // 64
+    for t in range(4):
+        for k in range(BASIS):
+            weights[k * SPAN + t * 64 : k * SPAN + (t + 1) * 64, :] = jnp.where(lane == t, mix_ref[k], jnp.zeros((), jnp.bfloat16))
+
+    def own_window(r, c):
+        window(x_ref[r], r + HALO)
+        return c
+
+    lax.fori_loop(0, rows, own_window, 0)
+    pl.semaphore_wait(barrier, 5)
+
+    def halo_copy(n):
+        return pltpu.make_async_remote_copy(
+            src_ref=x_ref.at[pl.ds(rows - HALO if n == 0 else 0, HALO)],
+            dst_ref=halo.at[n],
+            send_sem=halo_send.at[n],
+            recv_sem=halo_recv.at[n],
+            device_id={"lat": above if n == 0 else below},
+            device_id_type=pl.DeviceIdType.MESH,
+        )
+
+    for n in range(2):
+        halo_copy(n).start()
+
+    def chunk_copy(step, d):
+        return pltpu.make_async_remote_copy(
+            src_ref=send.at[partners[d], pl.ds(step * 2, 2)],
+            dst_ref=recv.at[me, pl.ds(step * 2, 2)],
+            send_sem=send_sem.at[d, step],
+            recv_sem=recv_sem.at[d, step],
+            device_id={"lon": partners[d]},
+            device_id_type=pl.DeviceIdType.MESH,
+        )
+
+    low = lax.broadcasted_iota(jnp.int32, (LINES, 128), 1) < 64
+
+    def body(idx, c):
+        step = lax.rem(idx + 1, steps)
+
+        @pl.when(idx == steps - 2)
+        def _():
+            for n in range(2):
+                halo_copy(n).wait()
+                for r in range(HALO):
+                    window(halo[n, r], r + n * (rows + HALO))
+
+        for r in range(STEP):
+            i = step * STEP + r
+            for k0 in range(0, BASIS, 3):
+                acc = None
+                for s in range(SLOTS):
+                    b = jnp.where(s < live_ref[i], band_ref[i, s], 8)
+                    part = lax.dot_general(
+                        bank[pl.ds(b * BASIS + k0, 3)].reshape(3 * LINES, SPAN),
+                        field[i + HALO + off_ref[i, s]],
+                        NT,
+                        preferred_element_type=jnp.float32,
+                    )
+                    acc = part if acc is None else acc + part
+                for k in range(3):
+                    quad[r * LINES : (r + 1) * LINES, (k0 + k) * SPAN : (k0 + k + 1) * SPAN] = acc[k * LINES : (k + 1) * LINES].astype(jnp.bfloat16)
+        mixed = jnp.dot(quad[...], weights[...], preferred_element_type=jnp.float32)
+        for p in range(STEP // 2):
+            even = mixed[2 * p * LINES : (2 * p + 1) * LINES]
+            odd = mixed[(2 * p + 1) * LINES : (2 * p + 2) * LINES]
+            for h in range(2):
+                e = even[:, h * 128 : (h + 1) * 128]
+                o = odd[:, h * 128 : (h + 1) * 128]
+                send[2 * h, step * 2 + p] = jnp.where(low, e, pltpu.roll(o, 64, 1)).astype(jnp.bfloat16)
+                send[2 * h + 1, step * 2 + p] = jnp.where(low, pltpu.roll(e, 64, 1), o).astype(jnp.bfloat16)
+        for d in range(3):
+            chunk_copy(step, d).start()
+        return c
+
+    lax.fori_loop(0, steps, body, 0)
+
+    def assemble(idx, c):
+        step = lax.rem(idx + 1, steps)
+        for d in range(3):
+            chunk_copy(step, d).wait()
+        recv[me, pl.ds(step * 2, 2)] = send[me, pl.ds(step * 2, 2)]
+        for p in range(STEP // 2):
+            pair = step * 2 + p
+            for h in range(2):
+                a = recv[2 * h, pair].astype(jnp.float32)
+                b = recv[2 * h + 1, pair].astype(jnp.float32)
+                out_ref[2 * pair, :, h * 128 : (h + 1) * 128] = jnp.where(low, a, pltpu.roll(b, 64, 1)).astype(jnp.bfloat16)[:TILE]
+                out_ref[2 * pair + 1, :, h * 128 : (h + 1) * 128] = jnp.where(low, pltpu.roll(a, 64, 1), b).astype(jnp.bfloat16)[:TILE]
+        return c
+
+    lax.fori_loop(0, steps, assemble, 0)
+
+
+def grouped_plan(band_field, offsets, live_counts, band_ids, tap_bank, mixing):
+    rows = band_field.shape[0]
+    steps = rows // STEP
+    taps = jnp.pad(tap_bank.transpose(1, 0, 2).astype(jnp.float32), ((0, 0), (0, 0), (0, 128))).reshape(72, SPAN)
+    own = jnp.tile(lax.dynamic_slice_in_dim(mixing, lax.axis_index("lon") * 64, 64, axis=2), (1, 1, 4))
+    sm = pl.BlockSpec(memory_space=pltpu.SMEM)
+    vm = pl.BlockSpec(memory_space=pltpu.VMEM)
+    return pl.pallas_call(
+        kernel,
+        out_shape=jax.ShapeDtypeStruct((rows, TILE, 256), jnp.bfloat16),
+        in_specs=[sm, sm, sm, vm, vm, vm],
+        out_specs=vm,
+        scratch_shapes=[
+            pltpu.VMEM((81, LINES, SPAN), jnp.bfloat16),
+            pltpu.VMEM((rows + 2 * HALO, SPAN, SPAN), jnp.bfloat16),
+            pltpu.VMEM((2, HALO, 64, 360), jnp.bfloat16),
+            pltpu.VMEM((BASIS * SPAN, SPAN), jnp.bfloat16),
+            pltpu.VMEM((STEP * LINES, BASIS * SPAN), jnp.bfloat16),
+            pltpu.VMEM((4, rows // 2, LINES, 128), jnp.bfloat16),
+            pltpu.VMEM((4, rows // 2, LINES, 128), jnp.bfloat16),
+            pltpu.SemaphoreType.DMA((3, steps)),
+            pltpu.SemaphoreType.DMA((3, steps)),
+            pltpu.SemaphoreType.DMA((2,)),
+            pltpu.SemaphoreType.DMA((2,)),
+        ],
+        compiler_params=pltpu.CompilerParams(vmem_limit_bytes=48 * 2**20, collective_id=0, has_side_effects=True),
+    )(offsets, live_counts, band_ids, band_field, taps, own)
+
+
 def solution(mesh):
+    def on_device(*args):
+        field = args[0]
+        grouped = field.shape[1] == 64 and field.shape[2] == 4 * TILE and mesh.shape["lon"] == 4 and mesh.shape["lat"] > 1
+        if grouped and field.shape[0] % STEP == 0 and field.shape[0] >= 4 * STEP:
+            return grouped_plan(*args)
+        return tiled_plan(*args)
+
     placed = (P(("ens", "lat"), "lon", None), P("lat", None), P("lat"), P("lat", None), P(), P())
     return jax.shard_map(
         on_device,

time: 905 us -> 40.7 us (0.04); the launches traced: 895 us -> 40.5 us
  loops' own time: 427 us -> 0 us
  local copies, waits for them, and re-layouts: 247 us -> 4.31 us
  matrix products: 177 us -> 0 us
  Pallas kernels: 0 us -> 35.4 us
  blocking collectives: 24.1 us -> 0 us
  other arithmetic: 11.9 us -> 0.73 us
    another operation x1 -> x0, loops' own time: 427 us -> none  [on_device(): return lax.map(one_row, (local_rows, offsets, live_counts, band_ids))]
    dot_general x160 -> x0, matrix products: 177 us -> none  [the longest x128 167 us: slot_term(): jnp.einsum('cj,kjl->kcl', source, matrix, preferred_element_type=jnp.floa...]
    gather x2 -> x0, local copies, waits for them, and re-layouts: 88.2 us -> none  [on_device(): picked = jnp.take(tap_bank, jnp.clip(distance, 0, 2 * REACH - 1), axis=2)]
    slice x67 -> x0, local copies, waits for them, and re-layouts: 45.3 us -> none  [the longest x32 19.4 us: one_row(): band_row[slot_index]]
    dynamic_slice x96 -> x1, local copies, waits for them, and re-layouts: 41.3 us -> 0.12 us  [grouped_plan(): lax.dynamic_slice_in_dim(mixing, lax.axis_index('lon') * 64, 64, axis=2)]
    pallas_call x0 -> x1, Pallas kernels: none -> 35.4 us  [grouped_plan(): pl.pallas_call(kernel, out_shape=jax.ShapeDtypeStruct((rows, TILE, 256),...]
    all_to_all x1 -> x0, blocking collectives: 24.1 us -> none  [on_device(): lax.all_to_all(band_field, 'lon', split_axis=2, concat_axis=1, tiled=True)]
    dynamic_update_slice x32 -> x0, local copies, waits for them, and re-layouts: 20.3 us -> none  [on_device(): return lax.map(one_row, (local_rows, offsets, live_counts, band_ids))]
  transfers between devices with their start and end apart: 4 -> 0, of which waited for: 0 -> 0; matrix products, arithmetic and copies ran while one was open for 12% -> 0% of each run, Pallas kernels for 0% -> 0%
where the time goes in v2:
time: 40.7 us; the launch traced here: 40.5 us
  Pallas kernels  35.4 us (87%)
  local copies, waits for them, and re-layouts  4.31 us (11%)
  other arithmetic  0.73 us (2%)
    pallas_call x1, Pallas kernels, grouped_plan(): pl.pallas_call(kernel, out_shape=jax.ShapeDtypeStruct((rows, TILE, 256),...  35.4 us
    pallas_call x1, local copies, waits for them, and re-layouts, grouped_plan(): pl.pallas_call(kernel, out_shape=jax.ShapeDtypeStruct((rows, TILE, 256),...  1.94 us
    unnamed x8, local copies, waits for them, and re-layouts  1.67 us

profile of v2, /device:TPU:0, one launch (start us, length us, event | category | flops | bytes accessed | tf_op | source)
XLA Modules:
  0.0 40.5 jit_solution(7330340193155449354)
XLA Ops:
  0.0 0.0 copy-start
  0.0 0.0 copy-start.2
  0.0 0.0 copy-start.1
  0.0 0.9 %copy.12.off_ref = s32[32,4]{1,0:T(8,128)S(1)} copy(s32[32,4]{0,1:T(4,128)} %param.7) | data formatting | bytes 1024 | tf_op args[1]
  0.9 0.8 %copy.13.band_ref = s32[32,4]{1,0:T(8,128)S(1)} copy(s32[32,4]{0,1:T(4,128)} %param.9) | data formatting | bytes 1024 | tf_op args[3]
  1.7 0.7 %pad_convert_fusion = f32[8,9,256]{2,0,1:T(8,128)S(1)} fusion(bf16[8,9,128]{2,0,1:T(8,128)(2,1)} %bitcast.1), kind=kLoop, calls=%fused_computation | loop fusion | flops 18432 | bytes 92160 | tf_op jit(solution)/shard_map/reshape | solution.py:203
  2.5 0.0 copy-done
  2.5 0.1 constant_dynamic-slice_fusion
  2.6 0.2 tile.4
  2.8 0.4 tile.10.mix_ref
  3.1 0.0 copy-done.2
  3.1 0.0 copy-done.1
  3.2 35.4 %shard_map.64 = bf16[32,90,256]{2,1,0:T(8,128)(2,1)S(1)} custom-call(s32[32,4]{1,0:T(8,128)S(1)} %copy.12.off_ref, s32[32]{0:T(128)S(1)} %copy-done.2, s32[32,4]{1,0:T(8,128)S(1)} %copy.13.band_ref, bf16[32,64,360]{2,1,0:T(8,128)(2,1)S(1)} %copy-done.1, f32[72,256]{1,0:T(8,128)S(1)} %reshape.12.taps_ref, bf16[9,64,256]{2,1,0:T(8,128)(2,1)S(1)} %tile.10.mix_ref), custom_call_target="tpu_custom_call" | custom-call | tf_op jit(solution)/shard_map/pallas_call | solution.py:207
  38.6 1.9 %copy.14 = bf16[32,90,256]{2,0,1:T(8,128)(2,1)} copy(bf16[32,90,256]{2,1,0:T(8,128)(2,1)S(1)} %shard_map.64) | data formatting | bytes 2949120 | tf_op jit(solution)/shard_map/pallas_call | solution.py:207
  (2 shorter events, 0.0 us)
Async XLA Ops:
  0.0 2.5 %copy-start = (bf16[9,64,256]{2,1,0:T(8,128)(2,1)S(1)}, bf16[9,64,256]{2,1,0:T(8,128)(2,1)}, u32[]{:S(2)}) copy-start(bf16[9,64,256]{2,1,0:T(8,128)(2,1)} %param.11) | copy-start | bytes 884740
  0.0 3.1 %copy-start.2 = (s32[32]{0:T(128)S(1)}, s32[32]{0:T(128)}, u32[]{:S(2)}) copy-start(s32[32]{0:T(128)} %live_ref.1) | copy-start | bytes 388
  0.0 3.1 %copy-start.1 = (bf16[32,64,360]{2,1,0:T(8,128)(2,1)S(1)}, bf16[32,64,360]{2,1,0:T(8,128)(2,1)}, u32[]{:S(2)}) copy-start(bf16[32,64,360]{2,1,0:T(8,128)(2,1)} %x_ref.1) | copy-start | bytes 4423684

commit v3 on v2

--- a/solution.py
+++ b/solution.py
@@ -96,23 +96,37 @@
                 piece = x[:, s : s + SPAN]
             field[slot, t * 64 : (t + 1) * 64, :] = piece
 
-    def bank_block(i, c):
-        line = jnp.broadcast_to(taps_ref[pl.ds(i, 1), :], (LINES, SPAN))
-        bank[i] = pltpu.roll(line, 0, 1, stride=1, stride_axis=0).astype(jnp.bfloat16)
-        return c
-
-    lax.fori_loop(0, 72, bank_block, 0, unroll=4)
+    def bank_blocks(k, c):
+        taps = taps_ref[k].astype(jnp.float32)
+        taps = jnp.concatenate([taps, jnp.zeros_like(taps)], axis=1)
+        for b in range(8):
+            line = jnp.broadcast_to(taps[b : b + 1], (16, SPAN))
+            base = pltpu.roll(line, 0, 1, stride=1, stride_axis=0).astype(jnp.bfloat16)
+            bank[b * BASIS + k, 0:16] = base
+            for j in range(1, LINES // 16):
+                bank[b * BASIS + k, 16 * j : 16 * (j + 1)] = jnp.concatenate([base[:, SPAN - 16 * j :], base[:, : SPAN - 16 * j]], axis=1)
+        return c
+
+    lax.fori_loop(0, BASIS, bank_blocks, 0)
     bank[72:81] = jnp.zeros((9, LINES, SPAN), jnp.bfloat16)
-    lane = lax.broadcasted_iota(jnp.int32, (64, SPAN), 1) // 64
-    for t in range(4):
-        for k in range(BASIS):
-            weights[k * SPAN + t * 64 : k * SPAN + (t + 1) * 64, :] = jnp.where(lane == t, mix_ref[k], jnp.zeros((), jnp.bfloat16))
+    half = lax.broadcasted_iota(jnp.int32, (64, 128), 1) < 64
+    nothing = jnp.zeros((64, 128), jnp.float32)
+    for k in range(BASIS):
+        mix = mix_ref[k].astype(jnp.float32)
+        near = jnp.where(me < 2, mix[:, :128], mix[:, 128:])
+        far = pltpu.roll(near, 64, 1)
+        even_group = lax.rem(me, 2) == 0
+        twice = jnp.where(half == even_group, near, far)
+        for t in range(4):
+            kept = jnp.where(half == (t % 2 == 0), twice, nothing)
+            sides = [kept, nothing] if t < 2 else [nothing, kept]
+            weights[k * SPAN + t * 64 : k * SPAN + (t + 1) * 64, :] = jnp.concatenate(sides, axis=1).astype(jnp.bfloat16)
 
     def own_window(r, c):
         window(x_ref[r], r + HALO)
         return c
 
-    lax.fori_loop(0, rows, own_window, 0)
+    lax.fori_loop(0, 2 * STEP + HALO, own_window, 0)
     pl.semaphore_wait(barrier, 5)
 
     def halo_copy(n):
@@ -155,16 +169,19 @@
             for k0 in range(0, BASIS, 3):
                 acc = None
                 for s in range(SLOTS):
-                    b = jnp.where(s < live_ref[i], band_ref[i, s], 8)
+                    b = jnp.where(s < live_ref[i], band_ref[i * SLOTS + s], 8)
                     part = lax.dot_general(
                         bank[pl.ds(b * BASIS + k0, 3)].reshape(3 * LINES, SPAN),
-                        field[i + HALO + off_ref[i, s]],
+                        field[i + HALO + off_ref[i * SLOTS + s]],
                         NT,
                         preferred_element_type=jnp.float32,
                     )
                     acc = part if acc is None else acc + part
                 for k in range(3):
                     quad[r * LINES : (r + 1) * LINES, (k0 + k) * SPAN : (k0 + k + 1) * SPAN] = acc[k * LINES : (k + 1) * LINES].astype(jnp.bfloat16)
+        for r in range(STEP):
+            ahead = jnp.minimum((idx + 2) * STEP + HALO + r, rows - 1)
+            window(x_ref[ahead], ahead + HALO)
         mixed = jnp.dot(quad[...], weights[...], preferred_element_type=jnp.float32)
         for p in range(STEP // 2):
             even = mixed[2 * p * LINES : (2 * p + 1) * LINES]
@@ -200,8 +217,6 @@
 def grouped_plan(band_field, offsets, live_counts, band_ids, tap_bank, mixing):
     rows = band_field.shape[0]
     steps = rows // STEP
-    taps = jnp.pad(tap_bank.transpose(1, 0, 2).astype(jnp.float32), ((0, 0), (0, 0), (0, 128))).reshape(72, SPAN)
-    own = jnp.tile(lax.dynamic_slice_in_dim(mixing, lax.axis_index("lon") * 64, 64, axis=2), (1, 1, 4))
     sm = pl.BlockSpec(memory_space=pltpu.SMEM)
     vm = pl.BlockSpec(memory_space=pltpu.VMEM)
     return pl.pallas_call(
@@ -223,7 +238,7 @@
             pltpu.SemaphoreType.DMA((2,)),
         ],
         compiler_params=pltpu.CompilerParams(vmem_limit_bytes=48 * 2**20, collective_id=0, has_side_effects=True),
-    )(offsets, live_counts, band_ids, band_field, taps, own)
+    )(offsets.reshape(-1), live_counts, band_ids.reshape(-1), band_field, tap_bank, mixing)
 
 
 def solution(mesh):

time: 40.7 us -> 39.9 us (0.980)
  Pallas kernels: 35.4 us -> 32.2 us
  local copies, waits for them, and re-layouts: 4.31 us -> 7.41 us
  other arithmetic: 0.73 us -> 0 us
    unnamed x8 -> x10, local copies, waits for them, and re-layouts: 1.67 us -> 5.27 us
    pallas_call x1, Pallas kernels: 35.4 us -> 32.2 us  [grouped_plan(): pl.pallas_call(kernel, out_shape=jax.ShapeDtypeStruct((rows, TILE, 256),...]
    reshape x1 -> x0, other arithmetic: 0.73 us -> none  [grouped_plan(): jnp.pad(tap_bank.transpose(1, 0, 2).astype(jnp.float32), ((0, 0), (0, 0),...]
    another operation x2 -> x0, local copies, waits for them, and re-layouts: 0.54 us -> none  [grouped_plan(): jnp.tile(lax.dynamic_slice_in_dim(mixing, lax.axis_index('lon') * 64, 64,...]
where the time goes in v3:
time: 39.9 us; the launch traced here: 39.6 us
  Pallas kernels  32.2 us (81%)
  local copies, waits for them, and re-layouts  7.41 us (19%)
    pallas_call x1, Pallas kernels, grouped_plan(): pl.pallas_call(kernel, out_shape=jax.ShapeDtypeStruct((rows, TILE, 256),...  32.2 us
    unnamed x10, local copies, waits for them, and re-layouts  5.27 us
    pallas_call x1, local copies, waits for them, and re-layouts, grouped_plan(): pl.pallas_call(kernel, out_shape=jax.ShapeDtypeStruct((rows, TILE, 256),...  1.93 us

profile of v3, /device:TPU:0, one launch (start us, length us, event | category | flops | bytes accessed | tf_op | source)
XLA Modules:
  0.0 39.6 jit_solution(13199709228862665982)
XLA Ops:
  0.0 0.8 %copy.10 = s32[32,4]{1,0:T(8,128)S(1)} copy(s32[32,4]{0,1:T(4,128)} %param.7) | data formatting | bytes 1024 | tf_op args[1]
  0.8 0.1 reshape.6.off_ref
  0.9 0.8 %copy.11 = s32[32,4]{1,0:T(8,128)S(1)} copy(s32[32,4]{0,1:T(4,128)} %param.9) | data formatting | bytes 1024 | tf_op args[3]
  1.6 0.1 reshape.7.band_ref
  1.7 0.0 copy-start
  1.8 1.4 %copy-done = bf16[32,64,360]{2,1,0:T(8,128)(2,1)S(1)} copy-done((bf16[32,64,360]{2,1,0:T(8,128)(2,1)S(1)}, bf16[32,64,360]{2,1,0:T(8,128)(2,1)}, u32[]{:S(2)}) %copy-start) | copy-done | bytes 1474584
  3.2 0.0 copy-start.1
  3.2 1.0 %copy-done.1 = bf16[9,64,256]{2,1,0:T(8,128)(2,1)S(1)} copy-done((bf16[9,64,256]{2,1,0:T(8,128)(2,1)S(1)}, bf16[9,64,256]{2,1,0:T(8,128)(2,1)}, u32[]{:S(2)}) %copy-start.1) | copy-done | bytes 294936
  4.1 0.0 copy-start.2
  4.1 0.7 %copy-done.2 = bf16[9,8,128]{2,1,0:T(8,128)(2,1)S(1)} copy-done((bf16[9,8,128]{2,1,0:T(8,128)(2,1)S(1)}, bf16[9,8,128]{2,1,0:T(8,128)(2,1)}, u32[]{:S(2)}) %copy-start.2) | copy-done | bytes 18456
  4.8 0.0 copy-start.3
  4.8 0.7 %copy-done.3 = s32[32]{0:T(128)S(1)} copy-done((s32[32]{0:T(128)S(1)}, s32[32]{0:T(128)}, u32[]{:S(2)}) %copy-start.3) | copy-done | bytes 152
  5.5 32.2 %shard_map.64 = bf16[32,90,256]{2,1,0:T(8,128)(2,1)S(1)} custom-call(s32[128]{0:T(128)S(1)} %reshape.6.off_ref, s32[32]{0:T(128)S(1)} %copy-done.3, s32[128]{0:T(128)S(1)} %reshape.7.band_ref, bf16[32,64,360]{2,1,0:T(8,128)(2,1)S(1)} %copy-done, bf16[9,8,128]{2,1,0:T(8,128)(2,1)S(1)} %copy-done.2, bf16[9,64,256]{2,1,0:T(8,128)(2,1)S(1)} %copy-done.1), custom_call_target="tpu_custom_call" | custom-call | tf_op jit(solution)/shard_map/pallas_call | solution.py:222
  37.7 1.9 %copy.12 = bf16[32,90,256]{2,0,1:T(8,128)(2,1)} copy(bf16[32,90,256]{2,1,0:T(8,128)(2,1)S(1)} %shard_map.64) | data formatting | bytes 2949120 | tf_op jit(solution)/shard_map/pallas_call | solution.py:222
Async XLA Ops:
  1.7 1.4 %copy-start = (bf16[32,64,360]{2,1,0:T(8,128)(2,1)S(1)}, bf16[32,64,360]{2,1,0:T(8,128)(2,1)}, u32[]{:S(2)}) copy-start(bf16[32,64,360]{2,1,0:T(8,128)(2,1)} %x_ref.1) | copy-start | bytes 4423684
  3.2 1.0 %copy-start.1 = (bf16[9,64,256]{2,1,0:T(8,128)(2,1)S(1)}, bf16[9,64,256]{2,1,0:T(8,128)(2,1)}, u32[]{:S(2)}) copy-start(bf16[9,64,256]{2,1,0:T(8,128)(2,1)} %mix_ref.1) | copy-start | bytes 884740
  4.1 0.7 %copy-start.2 = (bf16[9,8,128]{2,1,0:T(8,128)(2,1)S(1)}, bf16[9,8,128]{2,1,0:T(8,128)(2,1)}, u32[]{:S(2)}) copy-start(bf16[9,8,128]{2,1,0:T(8,128)(2,1)} %taps_ref.1) | copy-start | bytes 55300
  4.8 0.7 %copy-start.3 = (s32[32]{0:T(128)S(1)}, s32[32]{0:T(128)}, u32[]{:S(2)}) copy-start(s32[32]{0:T(128)} %live_ref.1) | copy-start | bytes 388

commit v4 on v3

--- a/solution.py
+++ b/solution.py
@@ -71,7 +71,7 @@
 LINES = 96
 
 
-def kernel(off_ref, live_ref, band_ref, x_ref, taps_ref, mix_ref, out_ref, bank, field, halo, weights, quad, send, recv, send_sem, recv_sem, halo_send, halo_recv):
+def kernel(off_in, live_in, band_in, x_in, taps_in, mix_in, out_hbm, off_ref, live_ref, band_ref, x_ref, taps_ref, mix_ref, load_sem, out_ref, store_sem, bank, field, halo, weights, quad, send, recv, send_sem, recv_sem, halo_send, halo_recv):
     me = lax.axis_index("lon")
     lat = lax.axis_index("lat")
     n_lat = lax.axis_size("lat")
@@ -81,6 +81,10 @@
     partners = [lax.rem(me + d, 4) for d in range(1, 4)]
     sources = [lax.rem(me + 4 - d, 4) for d in range(1, 4)]
 
+    pairs = [(taps_in, taps_ref), (mix_in, mix_ref), (x_in, x_ref), (off_in, off_ref), (live_in, live_ref), (band_in, band_ref)]
+    loads = [pltpu.make_async_copy(a, b, load_sem.at[n]) for n, (a, b) in enumerate(pairs)]
+    for load in loads:
+        load.start()
     barrier = pltpu.get_barrier_semaphore()
     for p in partners:
         pl.semaphore_signal(barrier, inc=1, device_id={"lon": p}, device_id_type=pl.DeviceIdType.MESH)
@@ -107,10 +111,12 @@
                 bank[b * BASIS + k, 16 * j : 16 * (j + 1)] = jnp.concatenate([base[:, SPAN - 16 * j :], base[:, : SPAN - 16 * j]], axis=1)
         return c
 
+    loads[0].wait()
     lax.fori_loop(0, BASIS, bank_blocks, 0)
     bank[72:81] = jnp.zeros((9, LINES, SPAN), jnp.bfloat16)
     half = lax.broadcasted_iota(jnp.int32, (64, 128), 1) < 64
     nothing = jnp.zeros((64, 128), jnp.float32)
+    loads[1].wait()
     for k in range(BASIS):
         mix = mix_ref[k].astype(jnp.float32)
         near = jnp.where(me < 2, mix[:, :128], mix[:, 128:])
@@ -126,6 +132,8 @@
         window(x_ref[r], r + HALO)
         return c
 
+    for load in loads[2:]:
+        load.wait()
     lax.fori_loop(0, 2 * STEP + HALO, own_window, 0)
     pl.semaphore_wait(barrier, 5)
 
@@ -169,10 +177,10 @@
             for k0 in range(0, BASIS, 3):
                 acc = None
                 for s in range(SLOTS):
-                    b = jnp.where(s < live_ref[i], band_ref[i * SLOTS + s], 8)
+                    b = jnp.where(s < live_ref[i], band_ref[s, i], 8)
                     part = lax.dot_general(
                         bank[pl.ds(b * BASIS + k0, 3)].reshape(3 * LINES, SPAN),
-                        field[i + HALO + off_ref[i * SLOTS + s]],
+                        field[i + HALO + off_ref[s, i]],
                         NT,
                         preferred_element_type=jnp.float32,
                     )
@@ -197,6 +205,10 @@
 
     lax.fori_loop(0, steps, body, 0)
 
+    def store(step):
+        cells = pl.ds(step * STEP, STEP)
+        return pltpu.make_async_copy(out_ref.at[cells], out_hbm.at[cells], store_sem.at[step])
+
     def assemble(idx, c):
         step = lax.rem(idx + 1, steps)
         for d in range(3):
@@ -209,22 +221,36 @@
                 b = recv[2 * h + 1, pair].astype(jnp.float32)
                 out_ref[2 * pair, :, h * 128 : (h + 1) * 128] = jnp.where(low, a, pltpu.roll(b, 64, 1)).astype(jnp.bfloat16)[:TILE]
                 out_ref[2 * pair + 1, :, h * 128 : (h + 1) * 128] = jnp.where(low, pltpu.roll(a, 64, 1), b).astype(jnp.bfloat16)[:TILE]
+        store(step).start()
+        return c
+
+    def finish(step, c):
+        store(step).wait()
         return c
 
     lax.fori_loop(0, steps, assemble, 0)
+    lax.fori_loop(0, steps, finish, 0)
 
 
 def grouped_plan(band_field, offsets, live_counts, band_ids, tap_bank, mixing):
     rows = band_field.shape[0]
     steps = rows // STEP
-    sm = pl.BlockSpec(memory_space=pltpu.SMEM)
-    vm = pl.BlockSpec(memory_space=pltpu.VMEM)
+    hbm = pl.BlockSpec(memory_space=pltpu.HBM)
     return pl.pallas_call(
         kernel,
         out_shape=jax.ShapeDtypeStruct((rows, TILE, 256), jnp.bfloat16),
-        in_specs=[sm, sm, sm, vm, vm, vm],
-        out_specs=vm,
+        in_specs=[hbm] * 6,
+        out_specs=hbm,
         scratch_shapes=[
+            pltpu.SMEM((SLOTS, rows), jnp.int32),
+            pltpu.SMEM((rows,), jnp.int32),
+            pltpu.SMEM((SLOTS, rows), jnp.int32),
+            pltpu.VMEM(band_field.shape, jnp.bfloat16),
+            pltpu.VMEM(tap_bank.shape, jnp.bfloat16),
+            pltpu.VMEM(mixing.shape, jnp.bfloat16),
+            pltpu.SemaphoreType.DMA((6,)),
+            pltpu.VMEM((rows, TILE, 256), jnp.bfloat16),
+            pltpu.SemaphoreType.DMA((steps,)),
             pltpu.VMEM((81, LINES, SPAN), jnp.bfloat16),
             pltpu.VMEM((rows + 2 * HALO, SPAN, SPAN), jnp.bfloat16),
             pltpu.VMEM((2, HALO, 64, 360), jnp.bfloat16),
@@ -237,8 +263,8 @@
             pltpu.SemaphoreType.DMA((2,)),
             pltpu.SemaphoreType.DMA((2,)),
         ],
-        compiler_params=pltpu.CompilerParams(vmem_limit_bytes=48 * 2**20, collective_id=0, has_side_effects=True),
-    )(offsets.reshape(-1), live_counts, band_ids.reshape(-1), band_field, tap_bank, mixing)
+        compiler_params=pltpu.CompilerParams(vmem_limit_bytes=63 * 2**20, collective_id=0, has_side_effects=True),
+    )(offsets.T, live_counts, band_ids.T, band_field, tap_bank, mixing)
 
 
 def solution(mesh):

time: 39.9 us -> 36.6 us (0.917)
  local copies, waits for them, and re-layouts: 7.41 us -> 3.34 us
  Pallas kernels: 32.2 us -> 33.1 us
    unnamed x10 -> x0, local copies, waits for them, and re-layouts: 5.27 us -> none
    pallas_call x1, local copies, waits for them, and re-layouts: 1.93 us -> 3.34 us  [grouped_plan(): pl.pallas_call(kernel, out_shape=jax.ShapeDtypeStruct((rows, TILE, 256),...]
    pallas_call x1, Pallas kernels: 32.2 us -> 33.1 us  [grouped_plan(): pl.pallas_call(kernel, out_shape=jax.ShapeDtypeStruct((rows, TILE, 256),...]
where the time goes in v4:
time: 36.6 us; the launch traced here: 36.5 us
  Pallas kernels  33.1 us (90%)
  local copies, waits for them, and re-layouts  3.34 us (9%)
    pallas_call x1, Pallas kernels, grouped_plan(): pl.pallas_call(kernel, out_shape=jax.ShapeDtypeStruct((rows, TILE, 256),...  33.1 us
    pallas_call x1, local copies, waits for them, and re-layouts, grouped_plan(): pl.pallas_call(kernel, out_shape=jax.ShapeDtypeStruct((rows, TILE, 256),...  3.34 us

profile of v4, /device:TPU:0, one launch (start us, length us, event | category | flops | bytes accessed | tf_op | source)
XLA Modules:
  0.0 36.5 jit_solution(7454218388783430619)
XLA Ops:
  0.0 33.1 %shard_map.64 = bf16[32,90,256]{2,1,0:T(8,128)(2,1)} custom-call(s32[4,32]{1,0:T(4,128)} %bitcast.2, s32[32]{0:T(128)} %live_in.1, s32[4,32]{1,0:T(4,128)} %bitcast.3, bf16[32,64,360]{2,1,0:T(8,128)(2,1)} %x_in.1, bf16[9,8,128]{2,1,0:T(8,128)(2,1)} %taps_in.1, bf16[9,64,256]{2,1,0:T(8,128)(2,1)} %mix_in.1), custom_call_target="tpu_custom_call" | custom-call | tf_op jit(solution)/shard_map/pallas_call | solution.py:239
  33.1 3.3 %copy.7 = bf16[32,90,256]{2,0,1:T(8,128)(2,1)} copy(bf16[32,90,256]{2,1,0:T(8,128)(2,1)} %shard_map.64) | data formatting | bytes 2949120 | tf_op jit(solution)/shard_map/pallas_call | solution.py:239
